TPU v7x, 128 devices: a whole 4x4x4 slice. The times are simulated.
128 devices in a mesh: wave: 8 (over y_hi, x), row: 16 (over y_lo, z, core).
Axes of the slice: x: 4, y: 4 (y_hi: 2, y_lo: 2; y = y_hi * 2 + y_lo), z: 4, core: 2. Of those that a mesh axis runs over, the one named last changes fastest.
Arguments:
- plane_waves: float32 [2, 8, 2048, 2048], P(None, 'wave', 'row'), may hold values from -6 to 6
- transmission: float32 [1, 2, 2048, 2048], P(None, None, 'row')
- wave_index: int32 [8, 2], P('wave'), may hold values from -32 to 31
- wave_weight: float32 [8], P('wave'), may hold values from 0.3 to 3
- wave_phase: float32 [8], P('wave'), may hold values from -3.140625 to 3.140625
- probe_pos: int32 [128, 2], replicated, may hold values from 0 to 2047, as said below
Outputs:
- diffraction: float32 [128, 128, 128], P('row', 'wave')
Inputs may be any that keep to these rules, and one draw needn't show every extreme that they name: `probe_pos`: the probes numbered j * 8 to (j + 1) * 8 - 1 have their grid row (first entry) in j * 128 to (j + 1) * 128 - 1; the second entry is the grid column.
All inputs are finite; a program needn't handle non-finite values.
Results may differ from a plain program's by a relative error of at most 0.0003.
Values sent between devices are 32-bit elements; how exact they have to be, the bound alone decides.
A program may use at most 64 MiB of HBM per device.

v0:
```python
import functools
import math

import jax
import jax.numpy as jnp
import ml_dtypes
import numpy as np
from jax import lax
from jax.experimental import pallas as pl
from jax.experimental.pallas import tpu as pltpu
from jax.sharding import PartitionSpec as P

MESH = pl.DeviceIdType.MESH
F32 = jnp.float32
BF16 = jnp.bfloat16

GRID = 2048
PARTS = 16
LANES = 128
WINDOW = 128
HALF = 64
FACTOR = 16
FRESNEL = 0.1
GROUPS = 11
KEEP = 8 * GROUPS
FIRST = -KEEP // 2
BLOCK = 2 * KEEP
DEPTH = PARTS * BLOCK
CHUNKS = ((0, 5), (5, 9), (9, 11))
PROBES = 8
NT = (((1,), (1,)), ((), ()))


def split_host(table):
    table = np.asarray(table, np.float32)
    high = table.astype(ml_dtypes.bfloat16)
    low = (table - high.astype(np.float32)).astype(ml_dtypes.bfloat16)
    return high, low


def host_tables(wave_count):
    lane = np.arange(LANES)
    freq = np.arange(KEEP) + FIRST
    group, part, member = np.meshgrid(np.arange(GROUPS), np.arange(2), np.arange(8), indexing="ij")
    row_freq = (group * 8 + member).reshape(-1) + FIRST
    row_imag = part.reshape(-1)

    angle = 2 * math.pi * (row_freq[:, None] * lane[None, :] % LANES) / LANES
    imag = row_imag[:, None] == 1
    forward_x = np.concatenate(
        [np.where(imag, -np.sin(angle), np.cos(angle)), np.where(imag, np.cos(angle), np.sin(angle))], axis=1
    )
    high, low = split_host(forward_x)
    forward_x = np.concatenate([high, high, low], axis=1)

    angle = 2 * math.pi * (lane[:, None] * freq[None, :] % LANES) / LANES
    pad = np.zeros((LANES, LANES - KEEP))
    cos = np.concatenate([np.cos(angle), pad], axis=1)
    sin = np.concatenate([np.sin(angle), pad], axis=1)
    forward_y = np.block([[cos, -sin], [sin, cos]])
    inverse_y = np.block([[cos.T, sin.T], [-sin.T, cos.T]])
    high, low = split_host(forward_y)
    forward_y = np.concatenate([high, high, low], axis=0)
    high, low = split_host(inverse_y)
    inverse_y = np.concatenate([high, high, low], axis=0)

    k1 = np.arange(PARTS)
    angle = -2 * math.pi * (k1[:, None] * lane[None, :]) / GRID
    twiddle = np.stack([np.cos(angle), np.sin(angle)], axis=1).astype(np.float32)
    twiddle = np.ascontiguousarray(np.broadcast_to(twiddle[:, :, None, :], (PARTS, 2, 8, LANES)))

    ky = k1[:, None] + 16 * np.concatenate([freq, np.full(LANES - KEEP, 4 * GRID)])[None, :]
    angle = -math.pi * FRESNEL / GRID * (ky.astype(np.float64) ** 2) - 2 * math.pi * (HALF * ky % GRID) / GRID
    inside = np.abs(ky) < GRID
    scale = inside / float(GRID * GRID)
    prop = np.stack([scale * np.cos(angle), scale * np.sin(angle)], axis=1).astype(np.float32)
    nine = np.where(inside, 9 * ky * ky, 2**30).astype(np.int32)[:, None, :]

    depth_kx, depth_imag = [], []
    for begin, end in CHUNKS:
        for source in range(PARTS):
            rows = slice(16 * begin, 16 * end)
            depth_kx.append(source + 16 * row_freq[rows])
            depth_imag.append(row_imag[rows])
    depth_kx = np.concatenate(depth_kx)
    depth_imag = np.concatenate(depth_imag)
    order = np.arange(WINDOW)
    mu = depth_kx[None, :] - 16 * order[:, None]
    dirichlet = np.zeros(mu.shape)
    for m in range(WINDOW // 2):
        dirichlet += 2 * np.cos(math.pi * ((2 * m + 1) * mu % (2 * GRID)) / GRID)
    dirichlet = dirichlet.astype(np.float32)
    fresnel = -math.pi * FRESNEL / GRID * depth_kx.astype(np.float64) ** 2
    fresnel = np.mod(fresnel + math.pi, 2 * math.pi) - math.pi
    phase_f = fresnel.astype(np.float32)[None, :]
    phase_i = np.stack([depth_kx, 1024 * depth_imag]).astype(np.int32)

    share = WINDOW // wave_count
    s, ri, q = np.meshgrid(np.arange(wave_count), np.arange(2), np.arange(share), indexing="ij")
    out_q = (s * share + q).reshape(-1)
    imag = ri.reshape(-1)[:, None] == 1
    angle = 2 * math.pi * (out_q[:, None] * lane[None, :] % LANES) / LANES
    last = np.concatenate(
        [np.where(imag, -np.sin(angle), np.cos(angle)), np.where(imag, np.cos(angle), np.sin(angle))], axis=1
    )
    high, low = split_host(last)
    last = np.concatenate([high, high, low], axis=1)
    return (forward_x, forward_y, inverse_y, twiddle, prop, nine, dirichlet, phase_f, phase_i, last)


def split(x):
    high = x.astype(BF16)
    low = (x - high.astype(F32)).astype(BF16)
    return high, low


def four(values, sign):
    (ar, ai), (br, bi), (cr, ci), (dr, di) = values
    s0r, s0i, s1r, s1i = ar + cr, ai + ci, ar - cr, ai - ci
    s2r, s2i, s3r, s3i = br + dr, bi + di, br - dr, bi - di
    if sign < 0:
        s3r, s3i = s3i, -s3r
        return [(s0r + s2r, s0i + s2i), (s1r + s3r, s1i + s3i), (s0r - s2r, s0i - s2i), (s1r - s3r, s1i - s3i)]
    return [(s0r + s2r, s0i + s2i), (s1r - s3i, s1i + s3r), (s0r - s2r, s0i - s2i), (s1r + s3i, s1i - s3r)]


def turn(value, power, sign):
    re, im = value
    power = power % 16
    if power == 0:
        return value
    if power == 4:
        return (im, -re) if sign < 0 else (-im, re)
    half = math.sqrt(0.5)
    if power == 2:
        if sign < 0:
            return (re + im) * half, (im - re) * half
        return (re - im) * half, (im + re) * half
    if power == 6:
        if sign < 0:
            return (im - re) * half, (re + im) * -half
        return (re + im) * -half, (re - im) * half
    c, s = math.cos(2 * math.pi * power / 16), sign * math.sin(2 * math.pi * power / 16)
    return re * c - im * s, re * s + im * c


def sixteen(values, sign):
    inner = [four([values[4 * a1 + a0] for a1 in range(4)], sign) for a0 in range(4)]
    out = [None] * 16
    for k0 in range(4):
        column = four([turn(inner[a0][k0], a0 * k0, sign) for a0 in range(4)], sign)
        for k1 in range(4):
            out[k0 + 4 * k1] = column[k1]
    return out


def cmul(ar, ai, br, bi):
    return ar * br - ai * bi, ar * bi + ai * br


def body(
    wave_count,
    pw_hbm, tr_hbm, fx_hbm, fy_hbm, iy_hbm, tw_hbm, py_hbm, nine_hbm, dk_hbm, pf_hbm, pi_hbm, last_hbm,
    pos_vec, pos_s, windex, wweight, wphase,
    out_ref,
    pw, tr, fx, fy, iy, tw, py, nine, dk, pf, pi, last,
    yx, send1, recv1, yy, send2, recv2, rows_re, rows_im, a_hi, a_lo, total, send3, recv3,
    load_sem, send1_sem, recv1_sem, send2_sem, recv2_sem, local_sem, send3_sem, recv3_sem,
):
    me = lax.axis_index("row")
    wv = lax.axis_index("wave")
    share = WINDOW // wave_count

    barrier = pltpu.get_barrier_semaphore()

    def greet_row(d, _):
        pl.semaphore_signal(barrier, inc=1, device_id={"row": lax.rem(me + d, PARTS)}, device_id_type=MESH)
        return 0

    def greet_wave(d, _):
        pl.semaphore_signal(barrier, inc=1, device_id={"wave": lax.rem(wv + d, wave_count)}, device_id_type=MESH)
        return 0

    lax.fori_loop(1, PARTS, greet_row, 0)
    if wave_count > 1:
        lax.fori_loop(1, wave_count, greet_wave, 0)

    tables = ((fx_hbm, fx), (tw_hbm, tw), (dk_hbm, dk), (pf_hbm, pf), (pi_hbm, pi), (fy_hbm, fy), (iy_hbm, iy),
              (py_hbm, py), (nine_hbm, nine), (last_hbm, last))
    loads = [pltpu.make_async_copy(pw_hbm.at[:, 0], pw, load_sem.at[0]),
             pltpu.make_async_copy(tr_hbm.at[0], tr, load_sem.at[1])]
    loads += [pltpu.make_async_copy(src, dst, load_sem.at[2 + n]) for n, (src, dst) in enumerate(tables)]
    for load in loads:
        load.start()
    for load in loads[:4]:
        load.wait()

    with jax.named_scope("column_transform"):
        def columns_16(r, _):
            rows = pl.ds(pl.multiple_of(r * 8, 8), 8)
            values = []
            for a in range(PARTS):
                cols = slice(a * LANES, (a + 1) * LANES)
                values.append(cmul(pw[0, rows, cols], pw[1, rows, cols], tr[0, rows, cols], tr[1, rows, cols]))
            for k, (re, im) in enumerate(sixteen(values, -1)):
                if k > 0:
                    re, im = cmul(re, im, tw[k, 0], tw[k, 1])
                yx[k, rows, :LANES] = re
                yx[k, rows, LANES:] = im
            return 0

        lax.fori_loop(0, LANES // 8, columns_16, 0)

    pl.semaphore_wait(barrier, PARTS - 1 + wave_count - 1)

    def copy1(c, peer):
        begin, end = CHUNKS[c]
        rows = pl.ds(16 * begin, 16 * (end - begin))
        return pltpu.make_async_remote_copy(
            src_ref=send1.at[peer, rows], dst_ref=recv1.at[me, rows],
            send_sem=send1_sem.at[c, peer], recv_sem=recv1_sem.at[c, me],
            device_id={"row": peer}, device_id_type=MESH,
        )

    def arrived1(c, source):
        begin, end = CHUNKS[c]
        rows = pl.ds(16 * begin, 16 * (end - begin))
        return pltpu.make_async_remote_copy(
            src_ref=send1.at[source, rows], dst_ref=recv1.at[source, rows],
            send_sem=send1_sem.at[c, source], recv_sem=recv1_sem.at[c, source],
            device_id={"row": source}, device_id_type=MESH,
        )

    with jax.named_scope("column_products"):
        def product(j):
            high, low = split(yx[j])
            return lax.dot_general(
                fx[...], jnp.concatenate([high, low, high], axis=1), NT, preferred_element_type=F32
            )

        def columns_128(d, _):
            j = lax.rem(me + d, PARTS)
            send1[j] = product(j)
            copy1(0, j).start()
            return 0

        lax.fori_loop(1, PARTS, columns_128, 0)
        for c in range(1, len(CHUNKS)):
            def more(d, _):
                copy1(c, lax.rem(me + d, PARTS)).start()
                return 0

            lax.fori_loop(1, PARTS, more, 0)
        recv1[me] = product(me)

    with jax.named_scope("window_weights"):
        for load in loads[4:]:
            load.wait()
        pos = pos_vec[pl.ds(pl.multiple_of(me * PROBES, PROBES), PROBES), :]
        r0, c0 = pos[:, 0:1], pos[:, 1:2]
        tilt = FACTOR * (r0 * windex[0, 0] + c0 * windex[0, 1])
        units = (2 * (c0 - HALF) + (WINDOW - 1)) * pi[0:1, :] + pi[1:2, :] - 2 * tilt
        units = jnp.bitwise_and(units, 2 * GRID - 1)
        angle = units.astype(F32) * (math.pi / GRID) + pf[...] + wphase[0]
        rows_re[...] = jnp.cos(angle) * wweight[0]
        rows_im[...] = jnp.sin(angle) * wweight[0]

        def weights_of(n, _):
            p, part = n // 8, lax.rem(n, 8)
            rows = pl.ds(pl.multiple_of(part * 16, 16), 16)
            rows2 = pl.ds(pl.multiple_of(part * 16 + WINDOW, 16), 16)
            base = dk[rows, :]
            high, low = split(base * rows_re[pl.ds(p, 1), :])
            a_hi[p, rows, :] = high
            a_lo[p, rows, :] = low
            high, low = split(base * rows_im[pl.ds(p, 1), :])
            a_hi[p, rows2, :] = high
            a_lo[p, rows2, :] = low
            return 0

        lax.fori_loop(0, PROBES * 8, weights_of, 0)

    def slot2(c, source):
        begin, end = CHUNKS[c]
        size = 16 * (end - begin)
        return pl.ds(pl.multiple_of(256 * begin + source * size, 16), size)

    def copy2(c, which, peer):
        begin, end = CHUNKS[c]
        rows = pl.ds(16 * begin, 16 * (end - begin))
        return pltpu.make_async_remote_copy(
            src_ref=send2.at[lax.rem(peer + which, PARTS), rows], dst_ref=recv2.at[which, slot2(c, me)],
            send_sem=send2_sem.at[c, which, peer], recv_sem=recv2_sem.at[c, which, me],
            device_id={"row": peer}, device_id_type=MESH,
        )

    def arrived2(c, which, source):
        begin, end = CHUNKS[c]
        rows = pl.ds(16 * begin, 16 * (end - begin))
        return pltpu.make_async_remote_copy(
            src_ref=send2.at[source, rows], dst_ref=recv2.at[which, slot2(c, source)],
            send_sem=send2_sem.at[c, which, source], recv_sem=recv2_sem.at[c, which, source],
            device_id={"row": source}, device_id_type=MESH,
        )

    def keep2(c, which):
        begin, end = CHUNKS[c]
        rows = pl.ds(16 * begin, 16 * (end - begin))
        return pltpu.make_async_copy(
            send2.at[lax.rem(me + which, PARTS), rows], recv2.at[which, slot2(c, me)], local_sem.at[c, which]
        )

    for c, (begin, end) in enumerate(CHUNKS):
        size = 8 * (end - begin)
        with jax.named_scope("wait_columns"):
            def wait1(d, _):
                arrived1(c, lax.rem(me + PARTS - d, PARTS)).wait_recv()
                return 0

            lax.fori_loop(1, PARTS, wait1, 0)

        with jax.named_scope("row_transform"):
            def rows_16(g, _):
                re_rows = pl.ds(pl.multiple_of(g * 16, 8), 8)
                im_rows = pl.ds(pl.multiple_of(g * 16 + 8, 8), 8)
                here = pl.ds(pl.multiple_of((g - begin) * 8, 8), 8)
                values = [(recv1[a, re_rows, :], recv1[a, im_rows, :]) for a in range(PARTS)]
                for k, (re, im) in enumerate(sixteen(values, -1)):
                    if k > 0:
                        re, im = cmul(re, im, tw[k, 0], tw[k, 1])
                    yy[k, here, :LANES] = re
                    yy[k, here, LANES:] = im
                return 0

            lax.fori_loop(begin, end, rows_16, 0)

            kx = me + 16 * (FIRST + 8 * begin + lax.broadcasted_iota(jnp.int32, (1, size, LANES), 1))
            limit = GRID * GRID - 9 * kx * kx

            def products(n, _):
                ks = pl.ds(n * 4, 4)
                y = yy[ks, :size, :].reshape(4 * size, 2 * LANES)
                high, low = split(y)
                f = jnp.dot(jnp.concatenate([high, low, high], axis=1), fy[...], preferred_element_type=F32)
                f = f.reshape(4, size, 2 * LANES)
                re, im = cmul(f[:, :, :LANES], f[:, :, LANES:], py[ks, 0:1, :], py[ks, 1:2, :])
                open_ = nine[ks] <= limit
                re = jnp.where(open_, re, 0.0)
                im = jnp.where(open_, im, 0.0)
                f = jnp.concatenate([re, im], axis=2).reshape(4 * size, 2 * LANES)
                high, low = split(f)
                f = jnp.dot(jnp.concatenate([high, low, high], axis=1), iy[...], preferred_element_type=F32)
                yy[ks, :size, :] = f.reshape(4, size, 2 * LANES)
                return 0

            lax.fori_loop(0, 4, products, 0)

            def rows_back(g, _):
                re_rows = pl.ds(pl.multiple_of(g * 16, 8), 8)
                im_rows = pl.ds(pl.multiple_of(g * 16 + 8, 8), 8)
                here = pl.ds(pl.multiple_of((g - begin) * 8, 8), 8)
                values = []
                for k in range(PARTS):
                    re, im = yy[k, here, :LANES], yy[k, here, LANES:]
                    if k > 0:
                        re, im = cmul(re, im, tw[k, 0], -tw[k, 1])
                    values.append((re, im))
                for a, (re, im) in enumerate(sixteen(values, 1)):
                    send2[a, re_rows, :] = re
                    send2[a, im_rows, :] = im
                return 0

            lax.fori_loop(begin, end, rows_back, 0)

        with jax.named_scope("send_rows"):
            def send(d, _):
                peer = lax.rem(me + d, PARTS)
                copy2(c, 0, peer).start()
                copy2(c, 1, peer).start()
                return 0

            lax.fori_loop(1, PARTS, send, 0)
            keep2(c, 0).start()
            keep2(c, 1).start()

    for c, (begin, end) in enumerate(CHUNKS):
        with jax.named_scope("wait_rows"):
            keep2(c, 0).wait()
            keep2(c, 1).wait()

            def wait2(d, _):
                source = lax.rem(me + PARTS - d, PARTS)
                arrived2(c, 0, source).wait_recv()
                arrived2(c, 1, source).wait_recv()
                return 0

            lax.fori_loop(1, PARTS, wait2, 0)
        with jax.named_scope("window_columns"):
            deep = slice(256 * begin, 256 * end)
            y = jnp.concatenate([recv2[0, deep, :], recv2[1, deep, :]], axis=1)
            high, low = split(y)

            def contract(p, _):
                t = jnp.dot(a_hi[p, :, deep], high, preferred_element_type=F32)
                t += jnp.dot(a_hi[p, :, deep], low, preferred_element_type=F32)
                t += jnp.dot(a_lo[p, :, deep], high, preferred_element_type=F32)
                if c == 0:
                    total[p] = t
                else:
                    total[p] += t
                return 0

            lax.fori_loop(0, PROBES, contract, 0)

    with jax.named_scope("window_rows"):
        lane = lax.broadcasted_iota(jnp.int32, (1, LANES), 1)

        def finish(p, _):
            offset = pos_s[me * PROBES + p, 0] - me * LANES
            t = total[p]
            u = jnp.where(lane >= offset, t[:, :LANES], t[:, LANES:])
            u = jnp.concatenate([u[:WINDOW], u[WINDOW:]], axis=1)
            high, low = split(u)
            v = lax.dot_general(
                last[...], jnp.concatenate([high, low, high], axis=1), NT, preferred_element_type=F32
            )
            send3[:, p] = v.reshape(wave_count, 2 * share, LANES)
            return 0

        lax.fori_loop(0, PROBES, finish, 0)

    with jax.named_scope("add_waves"):
        def copy3(peer, slot):
            return pltpu.make_async_remote_copy(
                src_ref=send3.at[peer], dst_ref=recv3.at[slot],
                send_sem=send3_sem.at[peer], recv_sem=recv3_sem.at[slot],
                device_id={"wave": peer}, device_id_type=MESH,
            )

        if wave_count > 1:
            def send_sum(d, _):
                copy3(lax.rem(wv + d, wave_count), wv).start()
                return 0

            lax.fori_loop(1, wave_count, send_sum, 0)
        recv3[wv] = send3[wv]
        if wave_count > 1:
            def wait3(d, _):
                source = lax.rem(wv + wave_count - d, wave_count)
                copy3(source, source).wait_recv()
                return 0

            lax.fori_loop(1, wave_count, wait3, 0)

        def intensity(p, _):
            v = recv3[0, p]
            for w in range(1, wave_count):
                v = v + recv3[w, p]
            re, im = v[:share], v[share:]
            out_ref[p] = (re * re + im * im) * (1.0 / (WINDOW * WINDOW * wave_count))
            return 0

        lax.fori_loop(0, PROBES, intensity, 0)

    with jax.named_scope("drain"):
        def drain(d, _):
            peer = lax.rem(me + d, PARTS)
            for c in range(len(CHUNKS)):
                copy1(c, peer).wait_send()
                copy2(c, 0, peer).wait_send()
                copy2(c, 1, peer).wait_send()
            return 0

        lax.fori_loop(1, PARTS, drain, 0)
        if wave_count > 1:
            def drain3(d, _):
                copy3(lax.rem(wv + d, wave_count), wv).wait_send()
                return 0

            lax.fori_loop(1, wave_count, drain3, 0)


def shards(wave_count, plane_waves, transmission, wave_index, wave_weight, wave_phase, probe_pos):
    tables = [jnp.asarray(t) for t in host_tables(wave_count)]
    share = WINDOW // wave_count
    rows = plane_waves.shape[2]
    chunks = len(CHUNKS)
    largest = max(8 * (end - begin) for begin, end in CHUNKS)
    any_ = pl.BlockSpec(memory_space=pl.ANY)
    vmem = pl.BlockSpec(memory_space=pltpu.VMEM)
    smem = pl.BlockSpec(memory_space=pltpu.SMEM)
    return pl.pallas_call(
        functools.partial(body, wave_count),
        out_shape=jax.ShapeDtypeStruct((PROBES, share, LANES), F32),
        in_specs=[any_] * 12 + [vmem] + [smem] * 4,
        out_specs=vmem,
        scratch_shapes=[
            pltpu.VMEM((2, rows, GRID), F32),
            pltpu.VMEM((2, rows, GRID), F32),
        ]
        + [pltpu.VMEM(t.shape, t.dtype) for t in tables]
        + [
            pltpu.VMEM((PARTS, LANES, 2 * LANES), F32),
            pltpu.VMEM((PARTS, BLOCK, LANES), F32),
            pltpu.VMEM((PARTS, BLOCK, LANES), F32),
            pltpu.VMEM((PARTS, largest, 2 * LANES), F32),
            pltpu.VMEM((PARTS, BLOCK, LANES), F32),
            pltpu.VMEM((2, DEPTH, LANES), F32),
            pltpu.VMEM((PROBES, DEPTH), F32),
            pltpu.VMEM((PROBES, DEPTH), F32),
            pltpu.VMEM((PROBES, 2 * WINDOW, DEPTH), BF16),
            pltpu.VMEM((PROBES, 2 * WINDOW, DEPTH), BF16),
            pltpu.VMEM((PROBES, 2 * WINDOW, 2 * LANES), F32),
            pltpu.VMEM((wave_count, PROBES, 2 * share, LANES), F32),
            pltpu.VMEM((wave_count, PROBES, 2 * share, LANES), F32),
            pltpu.SemaphoreType.DMA((2 + len(tables),)),
            pltpu.SemaphoreType.DMA((chunks, PARTS)),
            pltpu.SemaphoreType.DMA((chunks, PARTS)),
            pltpu.SemaphoreType.DMA((chunks, 2, PARTS)),
            pltpu.SemaphoreType.DMA((chunks, 2, PARTS)),
            pltpu.SemaphoreType.DMA((chunks, 2)),
            pltpu.SemaphoreType.DMA((wave_count,)),
            pltpu.SemaphoreType.DMA((wave_count,)),
        ],
        compiler_params=pltpu.CompilerParams(
            collective_id=0, has_side_effects=True, vmem_limit_bytes=60 * 1024 * 1024
        ),
    )(plane_waves, transmission, *tables, probe_pos, probe_pos, wave_index, wave_weight, wave_phase)


def solution(mesh):
    return jax.shard_map(
        functools.partial(shards, mesh.shape["wave"]),
        mesh=mesh,
        in_specs=(
            P(None, "wave", "row", None),
            P(None, None, "row", None),
            P("wave", None),
            P("wave"),
            P("wave"),
            P(),
        ),
        out_specs=P("row", "wave", None),
        check_vma=False,
    )
```

profile of v0, /device:TPU:1, one launch (start us, length us, event | category | flops | bytes accessed | tf_op | source)
XLA Modules:
  0.0 91.3 jit_solution(7992794048514404726)
XLA Ops:
  1.3 1.4 %copy.17.pos_vec.pos_s = s32[128,2]{1,0:T(8,128)} copy(s32[128,2]{0,1:T(2,128)} %param.21) | data formatting | bytes 2048 | tf_op args[5]
  2.7 87.1 %shard_map.154 = f32[8,16,128]{2,1,0:T(8,128)} custom-call(f32[2,1,128,2048]{3,2,1,0:T(8,128)} %pw_hbm.1, f32[1,2,128,2048]{3,2,1,0:T(8,128)} %tr_hbm.1, bf16[176,768]{1,0:T(8,128)(2,1)} %constant.20.clone.fx_hbm, bf16[768,256]{1,0:T(8,128)(2,1)} %constant.21.clone.fy_hbm, bf16[768,256]{1,0:T(8,128)(2,1)} %constant.22.clone.iy_hbm, ...), custom_call_target="tpu_custom_call" | custom-call | tf_op jit(solution)/shard_map/pallas_call | solution.py:492
  89.8 1.5 %copy.22 = f32[8,16,128]{2,1,0:T(8,128)} copy(f32[8,16,128]{2,1,0:T(8,128)} %shard_map.154) | data formatting | bytes 131072
where the time goes:
time: 92.6 us; the launch traced here: 91.3 us
  Pallas kernels  87.1 us (94%)
  local copies, waits for them, and re-layouts  2.89 us (3%)
  between operations  1.31 us (1%)
    pallas_call x1, Pallas kernels, shards(): pl.pallas_call(functools.partial(body, wave_count), out_shape=jax.ShapeDt...  87.1 us
    unnamed x2, local copies, waits for them, and re-layouts  2.89 us

commit v1 on v0

--- a/solution.py
+++ b/solution.py
@@ -21,6 +21,8 @@
 HALF = 64
 FACTOR = 16
 FRESNEL = 0.1
+ROWS_LOAD = 32
+BATCH = 2
 GROUPS = 11
 KEEP = 8 * GROUPS
 FIRST = -KEEP // 2
@@ -161,39 +163,61 @@
 def body(
     wave_count,
     pw_hbm, tr_hbm, fx_hbm, fy_hbm, iy_hbm, tw_hbm, py_hbm, nine_hbm, dk_hbm, pf_hbm, pi_hbm, last_hbm,
-    pos_vec, pos_s, windex, wweight, wphase,
+    pos_s, windex, wweight, wphase,
     out_ref,
     pw, tr, fx, fy, iy, tw, py, nine, dk, pf, pi, last,
     yx, send1, recv1, yy, send2, recv2, rows_re, rows_im, a_hi, a_lo, total, send3, recv3,
-    load_sem, send1_sem, recv1_sem, send2_sem, recv2_sem, local_sem, send3_sem, recv3_sem,
+    load_sem, rows_sem, send1_sem, recv1_sem, send2_sem, recv2_sem, forward_sem, local_sem, send3_sem, recv3_sem,
 ):
     me = lax.axis_index("row")
     wv = lax.axis_index("wave")
     share = WINDOW // wave_count
 
+    y_lo, z, core = me // 8, lax.rem(me // 2, 4), lax.rem(me, 2)
+    chip = me // 2
+    sibling = 2 * chip + 1 - core
+
+    def other_chip(n):
+        return lax.rem(y_lo + n // 4, 2) * 4 + lax.rem(z + n, 4)
+
+    def other_row(n):
+        return 2 * other_chip(lax.rem(n, 8)) + lax.rem(core + n // 8, 2)
+
+    def other_wave(n):
+        return lax.rem(wv + n, 4) + lax.rem(wv // 4 + n // 4, 2) * 4
+
     barrier = pltpu.get_barrier_semaphore()
 
     def greet_row(d, _):
-        pl.semaphore_signal(barrier, inc=1, device_id={"row": lax.rem(me + d, PARTS)}, device_id_type=MESH)
+        pl.semaphore_signal(barrier, inc=1, device_id={"row": other_row(d)}, device_id_type=MESH)
         return 0
 
     def greet_wave(d, _):
-        pl.semaphore_signal(barrier, inc=1, device_id={"wave": lax.rem(wv + d, wave_count)}, device_id_type=MESH)
+        pl.semaphore_signal(barrier, inc=1, device_id={"wave": other_wave(d)}, device_id_type=MESH)
         return 0
 
     lax.fori_loop(1, PARTS, greet_row, 0)
-    if wave_count > 1:
-        lax.fori_loop(1, wave_count, greet_wave, 0)
+    lax.fori_loop(1, wave_count, greet_wave, 0)
 
     tables = ((fx_hbm, fx), (tw_hbm, tw), (dk_hbm, dk), (pf_hbm, pf), (pi_hbm, pi), (fy_hbm, fy), (iy_hbm, iy),
               (py_hbm, py), (nine_hbm, nine), (last_hbm, last))
-    loads = [pltpu.make_async_copy(pw_hbm.at[:, 0], pw, load_sem.at[0]),
-             pltpu.make_async_copy(tr_hbm.at[0], tr, load_sem.at[1])]
-    loads += [pltpu.make_async_copy(src, dst, load_sem.at[2 + n]) for n, (src, dst) in enumerate(tables)]
-    for load in loads:
+    small = [pltpu.make_async_copy(src, dst, load_sem.at[n]) for n, (src, dst) in enumerate(tables)]
+
+    def load_rows(n):
+        rows = pl.ds(n * ROWS_LOAD, ROWS_LOAD)
+        return (
+            pltpu.make_async_copy(pw_hbm.at[:, 0, rows], pw.at[:, rows], rows_sem.at[0, n]),
+            pltpu.make_async_copy(tr_hbm.at[0, :, rows], tr.at[:, rows], rows_sem.at[1, n]),
+        )
+
+    small[1].start()
+    for n in range(LANES // ROWS_LOAD):
+        for load in load_rows(n):
+            load.start()
+    small[0].start()
+    for load in small[2:]:
         load.start()
-    for load in loads[:4]:
-        load.wait()
+    small[1].wait()
 
     with jax.named_scope("column_transform"):
         def columns_16(r, _):
@@ -209,7 +233,11 @@
                 yx[k, rows, LANES:] = im
             return 0
 
-        lax.fori_loop(0, LANES // 8, columns_16, 0)
+        for n in range(LANES // ROWS_LOAD):
+            for load in load_rows(n):
+                load.wait()
+            lax.fori_loop(n * ROWS_LOAD // 8, (n + 1) * ROWS_LOAD // 8, columns_16, 0)
+        small[0].wait()
 
     pl.semaphore_wait(barrier, PARTS - 1 + wave_count - 1)
 
@@ -239,7 +267,7 @@
             )
 
         def columns_128(d, _):
-            j = lax.rem(me + d, PARTS)
+            j = other_row(d)
             send1[j] = product(j)
             copy1(0, j).start()
             return 0
@@ -247,17 +275,21 @@
         lax.fori_loop(1, PARTS, columns_128, 0)
         for c in range(1, len(CHUNKS)):
             def more(d, _):
-                copy1(c, lax.rem(me + d, PARTS)).start()
+                copy1(c, other_row(d)).start()
                 return 0
 
             lax.fori_loop(1, PARTS, more, 0)
         recv1[me] = product(me)
 
     with jax.named_scope("window_weights"):
-        for load in loads[4:]:
+        for load in small[2:]:
             load.wait()
-        pos = pos_vec[pl.ds(pl.multiple_of(me * PROBES, PROBES), PROBES), :]
-        r0, c0 = pos[:, 0:1], pos[:, 1:2]
+        probe = lax.broadcasted_iota(jnp.int32, (PROBES, 1), 0)
+        r0 = jnp.zeros((PROBES, 1), jnp.int32)
+        c0 = jnp.zeros((PROBES, 1), jnp.int32)
+        for p in range(PROBES):
+            r0 = jnp.where(probe == p, pos_s[0, me * PROBES + p], r0)
+            c0 = jnp.where(probe == p, pos_s[1, me * PROBES + p], c0)
         tilt = FACTOR * (r0 * windex[0, 0] + c0 * windex[0, 1])
         units = (2 * (c0 - HALF) + (WINDOW - 1)) * pi[0:1, :] + pi[1:2, :] - 2 * tilt
         units = jnp.bitwise_and(units, 2 * GRID - 1)
@@ -285,36 +317,56 @@
         size = 16 * (end - begin)
         return pl.ds(pl.multiple_of(256 * begin + source * size, 16), size)
 
-    def copy2(c, which, peer):
+    def rows_of(c):
         begin, end = CHUNKS[c]
-        rows = pl.ds(16 * begin, 16 * (end - begin))
+        return pl.ds(16 * begin, 16 * (end - begin))
+
+    def copy2(c, block, which, target, sem):
         return pltpu.make_async_remote_copy(
-            src_ref=send2.at[lax.rem(peer + which, PARTS), rows], dst_ref=recv2.at[which, slot2(c, me)],
-            send_sem=send2_sem.at[c, which, peer], recv_sem=recv2_sem.at[c, which, me],
-            device_id={"row": peer}, device_id_type=MESH,
+            src_ref=send2.at[lax.rem(block, PARTS), rows_of(c)], dst_ref=recv2.at[which, slot2(c, me)],
+            send_sem=send2_sem.at[c, sem], recv_sem=recv2_sem.at[c, which, me],
+            device_id={"row": target}, device_id_type=MESH,
+        )
+
+    def copies2(c, n):
+        there = other_chip(n)
+        return (
+            copy2(c, 2 * there, 0, 2 * there, 3 * n),
+            copy2(c, 2 * there + 2, 1, 2 * there + 1, 3 * n + 1),
+            copy2(c, 2 * there + 1, 1 - core, 2 * there + core, 3 * n + 2),
+        )
+
+    def copy2_sibling(c):
+        return copy2(c, 2 * chip + 2 * (1 - core), 1 - core, sibling, 0)
+
+    def forward2(c, n):
+        source = 2 * other_chip(n) + core
+        return pltpu.make_async_remote_copy(
+            src_ref=recv2.at[1 - core, slot2(c, source)], dst_ref=recv2.at[core, slot2(c, source)],
+            send_sem=forward_sem.at[c, n], recv_sem=recv2_sem.at[c, core, source],
+            device_id={"row": sibling}, device_id_type=MESH,
         )
 
     def arrived2(c, which, source):
-        begin, end = CHUNKS[c]
-        rows = pl.ds(16 * begin, 16 * (end - begin))
         return pltpu.make_async_remote_copy(
-            src_ref=send2.at[source, rows], dst_ref=recv2.at[which, slot2(c, source)],
-            send_sem=send2_sem.at[c, which, source], recv_sem=recv2_sem.at[c, which, source],
-            device_id={"row": source}, device_id_type=MESH,
-        )
-
-    def keep2(c, which):
-        begin, end = CHUNKS[c]
-        rows = pl.ds(16 * begin, 16 * (end - begin))
+            src_ref=send2.at[source, rows_of(c)], dst_ref=recv2.at[which, slot2(c, source)],
+            send_sem=send2_sem.at[c, 0], recv_sem=recv2_sem.at[c, which, source],
+            device_id={"row": sibling}, device_id_type=MESH,
+        )
+
+    def keep2(c, which, block):
         return pltpu.make_async_copy(
-            send2.at[lax.rem(me + which, PARTS), rows], recv2.at[which, slot2(c, me)], local_sem.at[c, which]
-        )
+            send2.at[lax.rem(block, PARTS), rows_of(c)], recv2.at[which, slot2(c, me)], local_sem.at[c, which]
+        )
+
+    def keeps2(c):
+        return keep2(c, core, 2 * chip + 2 * core), keep2(c, 1 - core, 2 * chip + 1)
 
     for c, (begin, end) in enumerate(CHUNKS):
         size = 8 * (end - begin)
         with jax.named_scope("wait_columns"):
             def wait1(d, _):
-                arrived1(c, lax.rem(me + PARTS - d, PARTS)).wait_recv()
+                arrived1(c, other_row(d)).wait_recv()
                 return 0
 
             lax.fori_loop(1, PARTS, wait1, 0)
@@ -373,111 +425,136 @@
             lax.fori_loop(begin, end, rows_back, 0)
 
         with jax.named_scope("send_rows"):
-            def send(d, _):
-                peer = lax.rem(me + d, PARTS)
-                copy2(c, 0, peer).start()
-                copy2(c, 1, peer).start()
-                return 0
-
-            lax.fori_loop(1, PARTS, send, 0)
-            keep2(c, 0).start()
-            keep2(c, 1).start()
+            def send(n, _):
+                for copy in copies2(c, n):
+                    copy.start()
+                return 0
+
+            lax.fori_loop(1, PARTS // 2, send, 0)
+            copy2_sibling(c).start()
+            for copy in keeps2(c):
+                copy.start()
 
     for c, (begin, end) in enumerate(CHUNKS):
         with jax.named_scope("wait_rows"):
-            keep2(c, 0).wait()
-            keep2(c, 1).wait()
-
-            def wait2(d, _):
-                source = lax.rem(me + PARTS - d, PARTS)
-                arrived2(c, 0, source).wait_recv()
-                arrived2(c, 1, source).wait_recv()
-                return 0
-
-            lax.fori_loop(1, PARTS, wait2, 0)
+            for copy in keeps2(c):
+                copy.wait()
+            forward2(c, 0).start()
+
+            def shared(n, _):
+                arrived2(c, 1 - core, 2 * other_chip(n) + core).wait_recv()
+                forward2(c, n).start()
+                return 0
+
+            def exclusive(n, _):
+                arrived2(c, core, other_row(n)).wait_recv()
+                return 0
+
+            def forwarded(n, _):
+                arrived2(c, 1 - core, 2 * other_chip(n) + 1 - core).wait_recv()
+                return 0
+
+            lax.fori_loop(1, PARTS // 2, shared, 0)
+            lax.fori_loop(1, PARTS, exclusive, 0)
+            lax.fori_loop(0, PARTS // 2, forwarded, 0)
         with jax.named_scope("window_columns"):
             deep = slice(256 * begin, 256 * end)
             y = jnp.concatenate([recv2[0, deep, :], recv2[1, deep, :]], axis=1)
             high, low = split(y)
 
-            def contract(p, _):
+            def contract(p):
                 t = jnp.dot(a_hi[p, :, deep], high, preferred_element_type=F32)
                 t += jnp.dot(a_hi[p, :, deep], low, preferred_element_type=F32)
                 t += jnp.dot(a_lo[p, :, deep], high, preferred_element_type=F32)
+                return t
+
+            def partial(p, _):
                 if c == 0:
-                    total[p] = t
+                    total[p] = contract(p)
                 else:
-                    total[p] += t
-                return 0
-
-            lax.fori_loop(0, PROBES, contract, 0)
-
-    with jax.named_scope("window_rows"):
-        lane = lax.broadcasted_iota(jnp.int32, (1, LANES), 1)
-
-        def finish(p, _):
-            offset = pos_s[me * PROBES + p, 0] - me * LANES
-            t = total[p]
-            u = jnp.where(lane >= offset, t[:, :LANES], t[:, LANES:])
-            u = jnp.concatenate([u[:WINDOW], u[WINDOW:]], axis=1)
-            high, low = split(u)
-            v = lax.dot_general(
-                last[...], jnp.concatenate([high, low, high], axis=1), NT, preferred_element_type=F32
-            )
-            send3[:, p] = v.reshape(wave_count, 2 * share, LANES)
+                    total[p] += contract(p)
+                return 0
+
+            if c < len(CHUNKS) - 1:
+                lax.fori_loop(0, PROBES, partial, 0)
+                continue
+
+            lane = lax.broadcasted_iota(jnp.int32, (1, LANES), 1)
+
+            def copy3(b, peer, slot):
+                probes = pl.ds(b * BATCH, BATCH)
+                return pltpu.make_async_remote_copy(
+                    src_ref=send3.at[peer, probes], dst_ref=recv3.at[slot, probes],
+                    send_sem=send3_sem.at[b, peer], recv_sem=recv3_sem.at[b, slot],
+                    device_id={"wave": peer}, device_id_type=MESH,
+                )
+
+            def finish(p, _):
+                offset = pos_s[0, me * PROBES + p] - me * LANES
+                t = total[p] + contract(p)
+                u = jnp.where(lane >= offset, t[:, :LANES], t[:, LANES:])
+                u = jnp.concatenate([u[:WINDOW], u[WINDOW:]], axis=1)
+                u_high, u_low = split(u)
+                v = lax.dot_general(
+                    last[...], jnp.concatenate([u_high, u_low, u_high], axis=1), NT, preferred_element_type=F32
+                )
+                send3[:, p] = v.reshape(wave_count, 2 * share, LANES)
+                return 0
+
+            def batch(b, _):
+                lax.fori_loop(b * BATCH, (b + 1) * BATCH, finish, 0)
+
+                def send_sum(n, _):
+                    copy3(b, other_wave(n), wv).start()
+                    return 0
+
+                lax.fori_loop(1, wave_count, send_sum, 0)
+                return 0
+
+            lax.fori_loop(0, PROBES // BATCH, batch, 0)
+
+    with jax.named_scope("add_waves"):
+        def collect(b, _):
+            def wait3(n, _):
+                source = other_wave(n)
+                copy3(b, source, source).wait_recv()
+                return 0
+
+            lax.fori_loop(1, wave_count, wait3, 0)
+            probes = pl.ds(b * BATCH, BATCH)
+            v = send3[wv, probes]
+            for n in range(1, wave_count):
+                v = v + recv3[other_wave(n), probes]
+            re, im = v[:, :share], v[:, share:]
+            out_ref[probes] = (re * re + im * im) * (1.0 / (WINDOW * WINDOW * wave_count))
             return 0
 
-        lax.fori_loop(0, PROBES, finish, 0)
-
-    with jax.named_scope("add_waves"):
-        def copy3(peer, slot):
-            return pltpu.make_async_remote_copy(
-                src_ref=send3.at[peer], dst_ref=recv3.at[slot],
-                send_sem=send3_sem.at[peer], recv_sem=recv3_sem.at[slot],
-                device_id={"wave": peer}, device_id_type=MESH,
-            )
-
-        if wave_count > 1:
-            def send_sum(d, _):
-                copy3(lax.rem(wv + d, wave_count), wv).start()
-                return 0
-
-            lax.fori_loop(1, wave_count, send_sum, 0)
-        recv3[wv] = send3[wv]
-        if wave_count > 1:
-            def wait3(d, _):
-                source = lax.rem(wv + wave_count - d, wave_count)
-                copy3(source, source).wait_recv()
-                return 0
-
-            lax.fori_loop(1, wave_count, wait3, 0)
-
-        def intensity(p, _):
-            v = recv3[0, p]
-            for w in range(1, wave_count):
-                v = v + recv3[w, p]
-            re, im = v[:share], v[share:]
-            out_ref[p] = (re * re + im * im) * (1.0 / (WINDOW * WINDOW * wave_count))
+        lax.fori_loop(0, PROBES // BATCH, collect, 0)
+
+    with jax.named_scope("drain"):
+        def drain1(n, _):
+            for c in range(len(CHUNKS)):
+                copy1(c, other_row(n)).wait_send()
             return 0
 
-        lax.fori_loop(0, PROBES, intensity, 0)
-
-    with jax.named_scope("drain"):
-        def drain(d, _):
-            peer = lax.rem(me + d, PARTS)
+        def drain2(n, _):
             for c in range(len(CHUNKS)):
-                copy1(c, peer).wait_send()
-                copy2(c, 0, peer).wait_send()
-                copy2(c, 1, peer).wait_send()
+                for copy in copies2(c, n):
+                    copy.wait_send()
+                forward2(c, n).wait_send()
             return 0
 
-        lax.fori_loop(1, PARTS, drain, 0)
-        if wave_count > 1:
-            def drain3(d, _):
-                copy3(lax.rem(wv + d, wave_count), wv).wait_send()
-                return 0
-
-            lax.fori_loop(1, wave_count, drain3, 0)
+        def drain3(n, _):
+            for b in range(PROBES // BATCH):
+                copy3(b, other_wave(n), wv).wait_send()
+            return 0
+
+        lax.fori_loop(1, PARTS, drain1, 0)
+        lax.fori_loop(1, PARTS // 2, drain2, 0)
+        for c in range(len(CHUNKS)):
+            copy2_sibling(c).wait_send()
+            forward2(c, 0).wait_send()
+        lax.fori_loop(1, wave_count, drain3, 0)
 
 
 def shards(wave_count, plane_waves, transmission, wave_index, wave_weight, wave_phase, probe_pos):
@@ -492,7 +569,7 @@
     return pl.pallas_call(
         functools.partial(body, wave_count),
         out_shape=jax.ShapeDtypeStruct((PROBES, share, LANES), F32),
-        in_specs=[any_] * 12 + [vmem] + [smem] * 4,
+        in_specs=[any_] * 12 + [smem] * 4,
         out_specs=vmem,
         scratch_shapes=[
             pltpu.VMEM((2, rows, GRID), F32),
@@ -513,19 +590,21 @@
             pltpu.VMEM((PROBES, 2 * WINDOW, 2 * LANES), F32),
             pltpu.VMEM((wave_count, PROBES, 2 * share, LANES), F32),
             pltpu.VMEM((wave_count, PROBES, 2 * share, LANES), F32),
-            pltpu.SemaphoreType.DMA((2 + len(tables),)),
+            pltpu.SemaphoreType.DMA((len(tables),)),
+            pltpu.SemaphoreType.DMA((2, LANES // ROWS_LOAD)),
             pltpu.SemaphoreType.DMA((chunks, PARTS)),
             pltpu.SemaphoreType.DMA((chunks, PARTS)),
+            pltpu.SemaphoreType.DMA((chunks, 3 * PARTS // 2)),
             pltpu.SemaphoreType.DMA((chunks, 2, PARTS)),
-            pltpu.SemaphoreType.DMA((chunks, 2, PARTS)),
+            pltpu.SemaphoreType.DMA((chunks, PARTS // 2)),
             pltpu.SemaphoreType.DMA((chunks, 2)),
-            pltpu.SemaphoreType.DMA((wave_count,)),
-            pltpu.SemaphoreType.DMA((wave_count,)),
+            pltpu.SemaphoreType.DMA((PROBES // BATCH, wave_count)),
+            pltpu.SemaphoreType.DMA((PROBES // BATCH, wave_count)),
         ],
         compiler_params=pltpu.CompilerParams(
             collective_id=0, has_side_effects=True, vmem_limit_bytes=60 * 1024 * 1024
         ),
-    )(plane_waves, transmission, *tables, probe_pos, probe_pos, wave_index, wave_weight, wave_phase)
+    )(plane_waves, transmission, *tables, probe_pos.T, wave_index, wave_weight, wave_phase)
 
 
 def solution(mesh):

time: 92.6 us -> 78.7 us (0.85); the launches traced: 91.3 us -> 78.4 us
  Pallas kernels: 87.1 us -> 75.6 us
  local copies, waits for them, and re-layouts: 2.89 us -> 1.47 us
    pallas_call x1, Pallas kernels: 87.1 us -> 75.6 us  [shards(): pl.pallas_call(functools.partial(body, wave_count), out_shape=jax.ShapeDt...]
    unnamed x2 -> x1, local copies, waits for them, and re-layouts: 2.89 us -> 1.47 us
where the time goes in v1:
time: 78.7 us; the launch traced here: 78.4 us
  Pallas kernels  75.6 us (96%)
  local copies, waits for them, and re-layouts  1.47 us (2%)
  between operations  1.3 us (2%)
    pallas_call x1, Pallas kernels, shards(): pl.pallas_call(functools.partial(body, wave_count), out_shape=jax.ShapeDt...  75.6 us

profile of v1, /device:TPU:1, one launch (start us, length us, event | category | flops | bytes accessed | tf_op | source)
XLA Modules:
  0.0 78.4 jit_solution(7353577177828489284)
XLA Ops:
  1.3 75.6 %shard_map.154 = f32[8,16,128]{2,1,0:T(8,128)} custom-call(f32[2,1,128,2048]{3,2,1,0:T(8,128)} %pw_hbm.1, f32[1,2,128,2048]{3,2,1,0:T(8,128)} %tr_hbm.1, bf16[176,768]{1,0:T(8,128)(2,1)} %constant.20.clone.fx_hbm, bf16[768,256]{1,0:T(8,128)(2,1)} %constant.21.clone.fy_hbm, bf16[768,256]{1,0:T(8,128)(2,1)} %constant.22.clone.iy_hbm, ...), custom_call_target="tpu_custom_call" | custom-call | tf_op jit(solution)/shard_map/pallas_call | solution.py:569
  77.0 1.5 %copy.20 = f32[8,16,128]{2,1,0:T(8,128)} copy(f32[8,16,128]{2,1,0:T(8,128)} %shard_map.154) | data formatting | bytes 131072

commit v2 on v1

--- a/solution.py
+++ b/solution.py
@@ -28,8 +28,9 @@
 FIRST = -KEEP // 2
 BLOCK = 2 * KEEP
 DEPTH = PARTS * BLOCK
-CHUNKS = ((0, 5), (5, 9), (9, 11))
+CHUNKS = ((0, 4), (4, 8), (8, 11))
 PROBES = 8
+WAVE_ORDER = (4, 1, 3, 6, 2, 5, 7)
 NT = (((1,), (1,)), ((), ()))
 
 
@@ -163,8 +164,9 @@
 def body(
     wave_count,
     pw_hbm, tr_hbm, fx_hbm, fy_hbm, iy_hbm, tw_hbm, py_hbm, nine_hbm, dk_hbm, pf_hbm, pi_hbm, last_hbm,
+    pos_hbm, windex_hbm, wweight_hbm, wphase_hbm,
+    out_ref,
     pos_s, windex, wweight, wphase,
-    out_ref,
     pw, tr, fx, fy, iy, tw, py, nine, dk, pf, pi, last,
     yx, send1, recv1, yy, send2, recv2, rows_re, rows_im, a_hi, a_lo, total, send3, recv3,
     load_sem, rows_sem, send1_sem, recv1_sem, send2_sem, recv2_sem, forward_sem, local_sem, send3_sem, recv3_sem,
@@ -200,7 +202,8 @@
     lax.fori_loop(1, wave_count, greet_wave, 0)
 
     tables = ((fx_hbm, fx), (tw_hbm, tw), (dk_hbm, dk), (pf_hbm, pf), (pi_hbm, pi), (fy_hbm, fy), (iy_hbm, iy),
-              (py_hbm, py), (nine_hbm, nine), (last_hbm, last))
+              (py_hbm, py), (nine_hbm, nine), (last_hbm, last),
+              (pos_hbm, pos_s), (windex_hbm, windex), (wweight_hbm, wweight), (wphase_hbm, wphase))
     small = [pltpu.make_async_copy(src, dst, load_sem.at[n]) for n, (src, dst) in enumerate(tables)]
 
     def load_rows(n):
@@ -293,9 +296,9 @@
         tilt = FACTOR * (r0 * windex[0, 0] + c0 * windex[0, 1])
         units = (2 * (c0 - HALF) + (WINDOW - 1)) * pi[0:1, :] + pi[1:2, :] - 2 * tilt
         units = jnp.bitwise_and(units, 2 * GRID - 1)
-        angle = units.astype(F32) * (math.pi / GRID) + pf[...] + wphase[0]
-        rows_re[...] = jnp.cos(angle) * wweight[0]
-        rows_im[...] = jnp.sin(angle) * wweight[0]
+        angle = units.astype(F32) * (math.pi / GRID) + pf[...] + wphase[0, 0]
+        rows_re[...] = jnp.cos(angle) * wweight[0, 0]
+        rows_im[...] = jnp.sin(angle) * wweight[0, 0]
 
         def weights_of(n, _):
             p, part = n // 8, lax.rem(n, 8)
@@ -504,23 +507,38 @@
             def batch(b, _):
                 lax.fori_loop(b * BATCH, (b + 1) * BATCH, finish, 0)
 
-                def send_sum(n, _):
+                for n in WAVE_ORDER:
                     copy3(b, other_wave(n), wv).start()
-                    return 0
-
-                lax.fori_loop(1, wave_count, send_sum, 0)
                 return 0
 
             lax.fori_loop(0, PROBES // BATCH, batch, 0)
+
+    with jax.named_scope("drain"):
+        def drain1(n, _):
+            for c in range(len(CHUNKS)):
+                copy1(c, other_row(n)).wait_send()
+            return 0
+
+        def drain2(n, _):
+            for c in range(len(CHUNKS)):
+                for copy in copies2(c, n):
+                    copy.wait_send()
+                forward2(c, n).wait_send()
+            return 0
+
+        lax.fori_loop(1, PARTS, drain1, 0)
+        lax.fori_loop(1, PARTS // 2, drain2, 0)
+        for c in range(len(CHUNKS)):
+            copy2_sibling(c).wait_send()
+            forward2(c, 0).wait_send()
 
     with jax.named_scope("add_waves"):
         def collect(b, _):
-            def wait3(n, _):
+            for n in WAVE_ORDER:
+                copy3(b, other_wave(n), wv).wait_send()
+            for n in WAVE_ORDER:
                 source = other_wave(n)
                 copy3(b, source, source).wait_recv()
-                return 0
-
-            lax.fori_loop(1, wave_count, wait3, 0)
             probes = pl.ds(b * BATCH, BATCH)
             v = send3[wv, probes]
             for n in range(1, wave_count):
@@ -530,31 +548,6 @@
             return 0
 
         lax.fori_loop(0, PROBES // BATCH, collect, 0)
-
-    with jax.named_scope("drain"):
-        def drain1(n, _):
-            for c in range(len(CHUNKS)):
-                copy1(c, other_row(n)).wait_send()
-            return 0
-
-        def drain2(n, _):
-            for c in range(len(CHUNKS)):
-                for copy in copies2(c, n):
-                    copy.wait_send()
-                forward2(c, n).wait_send()
-            return 0
-
-        def drain3(n, _):
-            for b in range(PROBES // BATCH):
-                copy3(b, other_wave(n), wv).wait_send()
-            return 0
-
-        lax.fori_loop(1, PARTS, drain1, 0)
-        lax.fori_loop(1, PARTS // 2, drain2, 0)
-        for c in range(len(CHUNKS)):
-            copy2_sibling(c).wait_send()
-            forward2(c, 0).wait_send()
-        lax.fori_loop(1, wave_count, drain3, 0)
 
 
 def shards(wave_count, plane_waves, transmission, wave_index, wave_weight, wave_phase, probe_pos):
@@ -565,13 +558,16 @@
     largest = max(8 * (end - begin) for begin, end in CHUNKS)
     any_ = pl.BlockSpec(memory_space=pl.ANY)
     vmem = pl.BlockSpec(memory_space=pltpu.VMEM)
-    smem = pl.BlockSpec(memory_space=pltpu.SMEM)
     return pl.pallas_call(
         functools.partial(body, wave_count),
         out_shape=jax.ShapeDtypeStruct((PROBES, share, LANES), F32),
-        in_specs=[any_] * 12 + [smem] * 4,
+        in_specs=[any_] * 16,
         out_specs=vmem,
         scratch_shapes=[
+            pltpu.SMEM((2, PARTS * PROBES), jnp.int32),
+            pltpu.SMEM((1, 2), jnp.int32),
+            pltpu.SMEM((1, 1), F32),
+            pltpu.SMEM((1, 1), F32),
             pltpu.VMEM((2, rows, GRID), F32),
             pltpu.VMEM((2, rows, GRID), F32),
         ]
@@ -590,7 +586,7 @@
             pltpu.VMEM((PROBES, 2 * WINDOW, 2 * LANES), F32),
             pltpu.VMEM((wave_count, PROBES, 2 * share, LANES), F32),
             pltpu.VMEM((wave_count, PROBES, 2 * share, LANES), F32),
-            pltpu.SemaphoreType.DMA((len(tables),)),
+            pltpu.SemaphoreType.DMA((len(tables) + 4,)),
             pltpu.SemaphoreType.DMA((2, LANES // ROWS_LOAD)),
             pltpu.SemaphoreType.DMA((chunks, PARTS)),
             pltpu.SemaphoreType.DMA((chunks, PARTS)),
@@ -604,7 +600,7 @@
         compiler_params=pltpu.CompilerParams(
             collective_id=0, has_side_effects=True, vmem_limit_bytes=60 * 1024 * 1024
         ),
-    )(plane_waves, transmission, *tables, probe_pos.T, wave_index, wave_weight, wave_phase)
+    )(plane_waves, transmission, *tables, probe_pos.T, wave_index, wave_weight.reshape(1, 1), wave_phase.reshape(1, 1))
 
 
 def solution(mesh):

time: 78.7 us -> 77.1 us (0.980)
  Pallas kernels: 75.6 us -> 74.2 us
    pallas_call x1, Pallas kernels: 75.6 us -> 74.2 us  [shards(): pl.pallas_call(functools.partial(body, wave_count), out_shape=jax.ShapeDt...]
where the time goes in v2:
time: 77.1 us; the launch traced here: 76.9 us
  Pallas kernels  74.2 us (96%)
  local copies, waits for them, and re-layouts  1.47 us (2%)
  between operations  1.3 us (2%)
    pallas_call x1, Pallas kernels, shards(): pl.pallas_call(functools.partial(body, wave_count), out_shape=jax.ShapeDt...  74.2 us

profile of v2, /device:TPU:1, one launch (start us, length us, event | category | flops | bytes accessed | tf_op | source)
XLA Modules:
  0.0 76.9 jit_solution(14336382134598776831)
XLA Ops:
  1.3 74.2 %shard_map.154 = f32[8,16,128]{2,1,0:T(8,128)} custom-call(f32[2,1,128,2048]{3,2,1,0:T(8,128)} %pw_hbm.1, f32[1,2,128,2048]{3,2,1,0:T(8,128)} %tr_hbm.1, bf16[176,768]{1,0:T(8,128)(2,1)} %constant.20.clone.fx_hbm, bf16[768,256]{1,0:T(8,128)(2,1)} %constant.21.clone.fy_hbm, bf16[768,256]{1,0:T(8,128)(2,1)} %constant.22.clone.iy_hbm, ...), custom_call_target="tpu_custom_call" | custom-call | tf_op jit(solution)/shard_map/pallas_call | solution.py:561
  75.5 1.5 %copy.20 = f32[8,16,128]{2,1,0:T(8,128)} copy(f32[8,16,128]{2,1,0:T(8,128)} %shard_map.154) | data formatting | bytes 131072

commit v3 on v2

--- a/solution.py
+++ b/solution.py
@@ -28,7 +28,7 @@
 FIRST = -KEEP // 2
 BLOCK = 2 * KEEP
 DEPTH = PARTS * BLOCK
-CHUNKS = ((0, 4), (4, 8), (8, 11))
+CHUNKS = ((0, 5), (5, 9), (9, 11))
 PROBES = 8
 WAVE_ORDER = (4, 1, 3, 6, 2, 5, 7)
 NT = (((1,), (1,)), ((), ()))
@@ -79,14 +79,11 @@
     prop = np.stack([scale * np.cos(angle), scale * np.sin(angle)], axis=1).astype(np.float32)
     nine = np.where(inside, 9 * ky * ky, 2**30).astype(np.int32)[:, None, :]
 
-    depth_kx, depth_imag = [], []
+    depth_kx = []
     for begin, end in CHUNKS:
         for source in range(PARTS):
-            rows = slice(16 * begin, 16 * end)
-            depth_kx.append(source + 16 * row_freq[rows])
-            depth_imag.append(row_imag[rows])
+            depth_kx.append(source + 16 * freq[8 * begin:8 * end])
     depth_kx = np.concatenate(depth_kx)
-    depth_imag = np.concatenate(depth_imag)
     order = np.arange(WINDOW)
     mu = depth_kx[None, :] - 16 * order[:, None]
     dirichlet = np.zeros(mu.shape)
@@ -96,7 +93,7 @@
     fresnel = -math.pi * FRESNEL / GRID * depth_kx.astype(np.float64) ** 2
     fresnel = np.mod(fresnel + math.pi, 2 * math.pi) - math.pi
     phase_f = fresnel.astype(np.float32)[None, :]
-    phase_i = np.stack([depth_kx, 1024 * depth_imag]).astype(np.int32)
+    phase_i = depth_kx.astype(np.int32)[None, :]
 
     share = WINDOW // wave_count
     s, ri, q = np.meshgrid(np.arange(wave_count), np.arange(2), np.arange(share), indexing="ij")
@@ -294,7 +291,7 @@
             r0 = jnp.where(probe == p, pos_s[0, me * PROBES + p], r0)
             c0 = jnp.where(probe == p, pos_s[1, me * PROBES + p], c0)
         tilt = FACTOR * (r0 * windex[0, 0] + c0 * windex[0, 1])
-        units = (2 * (c0 - HALF) + (WINDOW - 1)) * pi[0:1, :] + pi[1:2, :] - 2 * tilt
+        units = (2 * (c0 - HALF) + (WINDOW - 1)) * pi[...] - 2 * tilt
         units = jnp.bitwise_and(units, 2 * GRID - 1)
         angle = units.astype(F32) * (math.pi / GRID) + pf[...] + wphase[0, 0]
         rows_re[...] = jnp.cos(angle) * wweight[0, 0]
@@ -302,15 +299,13 @@
 
         def weights_of(n, _):
             p, part = n // 8, lax.rem(n, 8)
-            rows = pl.ds(pl.multiple_of(part * 16, 16), 16)
-            rows2 = pl.ds(pl.multiple_of(part * 16 + WINDOW, 16), 16)
-            base = dk[rows, :]
-            high, low = split(base * rows_re[pl.ds(p, 1), :])
-            a_hi[p, rows, :] = high
-            a_lo[p, rows, :] = low
-            high, low = split(base * rows_im[pl.ds(p, 1), :])
-            a_hi[p, rows2, :] = high
-            a_lo[p, rows2, :] = low
+            base = dk[pl.ds(pl.multiple_of(part * 16, 16), 16), :]
+            rows = pl.ds(pl.multiple_of(n * 16, 16), 16)
+            re, im = rows_re[pl.ds(p, 1), :], rows_im[pl.ds(p, 1), :]
+            for kind, factor in enumerate((re, re + im, im - re)):
+                high, low = split(base * factor)
+                a_hi[kind, rows, :] = high
+                a_lo[kind, rows, :] = low
             return 0
 
         lax.fori_loop(0, PROBES * 8, weights_of, 0)
@@ -461,25 +456,37 @@
             lax.fori_loop(1, PARTS, exclusive, 0)
             lax.fori_loop(0, PARTS // 2, forwarded, 0)
         with jax.named_scope("window_columns"):
-            deep = slice(256 * begin, 256 * end)
-            y = jnp.concatenate([recv2[0, deep, :], recv2[1, deep, :]], axis=1)
-            high, low = split(y)
-
-            def contract(p):
-                t = jnp.dot(a_hi[p, :, deep], high, preferred_element_type=F32)
-                t += jnp.dot(a_hi[p, :, deep], low, preferred_element_type=F32)
-                t += jnp.dot(a_lo[p, :, deep], high, preferred_element_type=F32)
-                return t
-
-            def partial(p, _):
-                if c == 0:
-                    total[p] = contract(p)
-                else:
-                    total[p] += contract(p)
+            deep = slice(128 * begin, 128 * end)
+            y = jnp.concatenate(
+                [recv2[0, 256 * begin:256 * end, :], recv2[1, 256 * begin:256 * end, :]], axis=1
+            ).reshape(16 * (end - begin), 2, 8, 2 * LANES)
+            size = 128 * (end - begin)
+            y_re, y_im = y[:, 0].reshape(size, 2 * LANES), y[:, 1].reshape(size, 2 * LANES)
+            stacks = []
+            for part in (y_re + y_im, y_im, y_re):
+                high, low = split(part)
+                stacks.append(jnp.concatenate([high, low, high], axis=0))
+
+            def contract(b):
+                rows = pl.ds(pl.multiple_of(b * BATCH * WINDOW, 16), BATCH * WINDOW)
+                sums = []
+                for kind in range(3):
+                    high = a_hi[kind, rows, deep]
+                    both = jnp.concatenate([high, high, a_lo[kind, rows, deep]], axis=1)
+                    sums.append(jnp.dot(both, stacks[kind], preferred_element_type=F32))
+                re, im = sums[0] - sums[1], sums[0] + sums[2]
+                if c > 0:
+                    re, im = re + total[0, rows, :], im + total[1, rows, :]
+                return rows, re, im
+
+            def partial(b, _):
+                rows, re, im = contract(b)
+                total[0, rows, :] = re
+                total[1, rows, :] = im
                 return 0
 
             if c < len(CHUNKS) - 1:
-                lax.fori_loop(0, PROBES, partial, 0)
+                lax.fori_loop(0, PROBES // BATCH, partial, 0)
                 continue
 
             lane = lax.broadcasted_iota(jnp.int32, (1, LANES), 1)
@@ -492,20 +499,20 @@
                     device_id={"wave": peer}, device_id_type=MESH,
                 )
 
-            def finish(p, _):
-                offset = pos_s[0, me * PROBES + p] - me * LANES
-                t = total[p] + contract(p)
-                u = jnp.where(lane >= offset, t[:, :LANES], t[:, LANES:])
-                u = jnp.concatenate([u[:WINDOW], u[WINDOW:]], axis=1)
-                u_high, u_low = split(u)
-                v = lax.dot_general(
-                    last[...], jnp.concatenate([u_high, u_low, u_high], axis=1), NT, preferred_element_type=F32
-                )
-                send3[:, p] = v.reshape(wave_count, 2 * share, LANES)
-                return 0
-
             def batch(b, _):
-                lax.fori_loop(b * BATCH, (b + 1) * BATCH, finish, 0)
+                _, re, im = contract(b)
+                for n in range(BATCH):
+                    p = b * BATCH + n
+                    offset = pos_s[0, me * PROBES + p] - me * LANES
+                    here = slice(n * WINDOW, (n + 1) * WINDOW)
+                    u = jnp.concatenate(
+                        [jnp.where(lane >= offset, t[here, :LANES], t[here, LANES:]) for t in (re, im)], axis=1
+                    )
+                    u_high, u_low = split(u)
+                    v = lax.dot_general(
+                        last[...], jnp.concatenate([u_high, u_low, u_high], axis=1), NT, preferred_element_type=F32
+                    )
+                    send3[:, p] = v.reshape(wave_count, 2 * share, LANES)
 
                 for n in WAVE_ORDER:
                     copy3(b, other_wave(n), wv).start()
@@ -579,11 +586,11 @@
             pltpu.VMEM((PARTS, largest, 2 * LANES), F32),
             pltpu.VMEM((PARTS, BLOCK, LANES), F32),
             pltpu.VMEM((2, DEPTH, LANES), F32),
-            pltpu.VMEM((PROBES, DEPTH), F32),
-            pltpu.VMEM((PROBES, DEPTH), F32),
-            pltpu.VMEM((PROBES, 2 * WINDOW, DEPTH), BF16),
-            pltpu.VMEM((PROBES, 2 * WINDOW, DEPTH), BF16),
-            pltpu.VMEM((PROBES, 2 * WINDOW, 2 * LANES), F32),
+            pltpu.VMEM((PROBES, DEPTH // 2), F32),
+            pltpu.VMEM((PROBES, DEPTH // 2), F32),
+            pltpu.VMEM((3, PROBES * WINDOW, DEPTH // 2), BF16),
+            pltpu.VMEM((3, PROBES * WINDOW, DEPTH // 2), BF16),
+            pltpu.VMEM((2, PROBES * WINDOW, 2 * LANES), F32),
             pltpu.VMEM((wave_count, PROBES, 2 * share, LANES), F32),
             pltpu.VMEM((wave_count, PROBES, 2 * share, LANES), F32),
             pltpu.SemaphoreType.DMA((len(tables) + 4,)),

time: 77.1 us -> 76 us (0.986)
  Pallas kernels: 74.2 us -> 73.1 us
    pallas_call x1, Pallas kernels: 74.2 us -> 73.1 us  [shards(): pl.pallas_call(functools.partial(body, wave_count), out_shape=jax.ShapeDt...]
where the time goes in v3:
time: 76 us; the launch traced here: 75.9 us
  Pallas kernels  73.1 us (96%)
  local copies, waits for them, and re-layouts  1.47 us (2%)
  between operations  1.3 us (2%)
    pallas_call x1, Pallas kernels, shards(): pl.pallas_call(functools.partial(body, wave_count), out_shape=jax.ShapeDt...  73.1 us

profile of v3, /device:TPU:1, one launch (start us, length us, event | category | flops | bytes accessed | tf_op | source)
XLA Modules:
  0.0 75.9 jit_solution(14896979082373540625)
XLA Ops:
  1.3 73.1 %shard_map.154 = f32[8,16,128]{2,1,0:T(8,128)} custom-call(f32[2,1,128,2048]{3,2,1,0:T(8,128)} %pw_hbm.1, f32[1,2,128,2048]{3,2,1,0:T(8,128)} %tr_hbm.1, bf16[176,768]{1,0:T(8,128)(2,1)} %constant.20.clone.fx_hbm, bf16[768,256]{1,0:T(8,128)(2,1)} %constant.21.clone.fy_hbm, bf16[768,256]{1,0:T(8,128)(2,1)} %constant.22.clone.iy_hbm, ...), custom_call_target="tpu_custom_call" | custom-call | tf_op jit(solution)/shard_map/pallas_call | solution.py:568
  74.4 1.5 %copy.20 = f32[8,16,128]{2,1,0:T(8,128)} copy(f32[8,16,128]{2,1,0:T(8,128)} %shard_map.154) | data formatting | bytes 131072

commit v4 on v3

--- a/solution.py
+++ b/solution.py
@@ -31,6 +31,7 @@
 CHUNKS = ((0, 5), (5, 9), (9, 11))
 PROBES = 8
 WAVE_ORDER = (4, 1, 3, 6, 2, 5, 7)
+ROUTED = (2, 2)
 NT = (((1,), (1,)), ((), ()))
 
 
@@ -165,8 +166,8 @@
     out_ref,
     pos_s, windex, wweight, wphase,
     pw, tr, fx, fy, iy, tw, py, nine, dk, pf, pi, last,
-    yx, send1, recv1, yy, send2, recv2, rows_re, rows_im, a_hi, a_lo, total, send3, recv3,
-    load_sem, rows_sem, send1_sem, recv1_sem, send2_sem, recv2_sem, forward_sem, local_sem, send3_sem, recv3_sem,
+    yx, send1, recv1, yy, send2, recv2, rows_re, rows_im, a_hi, a_lo, total, send3, recv3, recv_y, sum_y, back_y, recv_x, sum_x, back_x,
+    load_sem, rows_sem, send1_sem, recv1_sem, send2_sem, recv2_sem, forward_sem, local_sem, send3_sem, recv3_sem, send4_sem, recv4_sem,
 ):
     me = lax.axis_index("row")
     wv = lax.axis_index("wave")
@@ -433,6 +434,54 @@
             for copy in keeps2(c):
                 copy.start()
 
+    x, y_hi = lax.rem(wv, 4), wv // 4
+    n_y, n_x = ROUTED
+    n_d = PROBES - n_y - n_x
+
+    def wave_of(step_y, step_x):
+        return lax.rem(y_hi + step_y, 2) * 4 + lax.rem(x + step_x, 4)
+
+    def copy_y(_):
+        far = 1 - y_hi
+        return pltpu.make_async_remote_copy(
+            src_ref=send3.at[far, :, pl.ds(0, n_y)], dst_ref=recv_y,
+            send_sem=send4_sem.at[0], recv_sem=recv4_sem.at[0],
+            device_id={"wave": wave_of(1, 0)}, device_id_type=MESH,
+        )
+
+    def copy_y_back(n):
+        to = lax.rem(x + n, 4)
+        return pltpu.make_async_remote_copy(
+            src_ref=sum_y.at[to], dst_ref=back_y.at[3 - n],
+            send_sem=send4_sem.at[n], recv_sem=recv4_sem.at[4 - n],
+            device_id={"wave": wave_of(0, n)}, device_id_type=MESH,
+        )
+
+    def copy_x(n):
+        to = lax.rem(x + n, 4)
+        return pltpu.make_async_remote_copy(
+            src_ref=send3.at[:, to, pl.ds(n_y, n_x)], dst_ref=recv_x.at[3 - n],
+            send_sem=send4_sem.at[3 + n], recv_sem=recv4_sem.at[7 - n],
+            device_id={"wave": wave_of(0, n)}, device_id_type=MESH,
+        )
+
+    def copy_x_back(_):
+        far = 1 - y_hi
+        return pltpu.make_async_remote_copy(
+            src_ref=sum_x.at[far], dst_ref=back_x,
+            send_sem=send4_sem.at[7], recv_sem=recv4_sem.at[7],
+            device_id={"wave": wave_of(1, 0)}, device_id_type=MESH,
+        )
+
+    def copy_d(n):
+        to_y, to_x = lax.rem(y_hi + n // 4, 2), lax.rem(x + n, 4)
+        slot = 4 * (n // 4) + lax.rem(4 - lax.rem(n, 4), 4)
+        return pltpu.make_async_remote_copy(
+            src_ref=send3.at[to_y, to_x, pl.ds(n_y + n_x, n_d)], dst_ref=recv3.at[slot],
+            send_sem=send3_sem.at[n], recv_sem=recv3_sem.at[slot],
+            device_id={"wave": wave_of(n // 4, n)}, device_id_type=MESH,
+        )
+
     for c, (begin, end) in enumerate(CHUNKS):
         with jax.named_scope("wait_rows"):
             for copy in keeps2(c):
@@ -491,14 +540,6 @@
 
             lane = lax.broadcasted_iota(jnp.int32, (1, LANES), 1)
 
-            def copy3(b, peer, slot):
-                probes = pl.ds(b * BATCH, BATCH)
-                return pltpu.make_async_remote_copy(
-                    src_ref=send3.at[peer, probes], dst_ref=recv3.at[slot, probes],
-                    send_sem=send3_sem.at[b, peer], recv_sem=recv3_sem.at[b, slot],
-                    device_id={"wave": peer}, device_id_type=MESH,
-                )
-
             def batch(b, _):
                 _, re, im = contract(b)
                 for n in range(BATCH):
@@ -512,13 +553,27 @@
                     v = lax.dot_general(
                         last[...], jnp.concatenate([u_high, u_low, u_high], axis=1), NT, preferred_element_type=F32
                     )
-                    send3[:, p] = v.reshape(wave_count, 2 * share, LANES)
-
-                for n in WAVE_ORDER:
-                    copy3(b, other_wave(n), wv).start()
-                return 0
-
-            lax.fori_loop(0, PROBES // BATCH, batch, 0)
+                    send3[:, :, p] = v.reshape(2, 4, 2 * share, LANES)
+                return 0
+
+            lax.fori_loop(0, n_y // BATCH, batch, 0)
+            copy_y(0).start()
+            lax.fori_loop(n_y // BATCH, (n_y + n_x) // BATCH, batch, 0)
+            for n in (1, 3, 2):
+                copy_x(n).start()
+            lax.fori_loop((n_y + n_x) // BATCH, PROBES // BATCH, batch, 0)
+            for n in WAVE_ORDER:
+                copy_d(n).start()
+
+    with jax.named_scope("first_sums"):
+        copy_y(0).wait_recv()
+        sum_y[...] = send3[y_hi, :, :n_y] + recv_y[...]
+        for n in (1, 3, 2):
+            copy_y_back(n).start()
+        for n in (1, 3, 2):
+            copy_x(n).wait_recv()
+        sum_x[...] = send3[:, x, n_y:n_y + n_x] + recv_x[0] + recv_x[1] + recv_x[2]
+        copy_x_back(0).start()
 
     with jax.named_scope("drain"):
         def drain1(n, _):
@@ -539,22 +594,31 @@
             copy2_sibling(c).wait_send()
             forward2(c, 0).wait_send()
 
+        for n in (1, 2, 3):
+            copy_x(n).wait_send()
+            copy_y_back(n).wait_send()
+        copy_y(0).wait_send()
+        for n in WAVE_ORDER:
+            copy_d(n).wait_send()
+        copy_x_back(0).wait_send()
+
     with jax.named_scope("add_waves"):
-        def collect(b, _):
-            for n in WAVE_ORDER:
-                copy3(b, other_wave(n), wv).wait_send()
-            for n in WAVE_ORDER:
-                source = other_wave(n)
-                copy3(b, source, source).wait_recv()
-            probes = pl.ds(b * BATCH, BATCH)
-            v = send3[wv, probes]
-            for n in range(1, wave_count):
-                v = v + recv3[other_wave(n), probes]
+        def store(first, v):
             re, im = v[:, :share], v[:, share:]
-            out_ref[probes] = (re * re + im * im) * (1.0 / (WINDOW * WINDOW * wave_count))
-            return 0
-
-        lax.fori_loop(0, PROBES // BATCH, collect, 0)
+            out_ref[first:first + v.shape[0]] = (re * re + im * im) * (1.0 / (WINDOW * WINDOW * wave_count))
+
+        for n in WAVE_ORDER:
+            copy_d(n).wait_recv()
+        v = send3[y_hi, x, n_y + n_x:]
+        for n in WAVE_ORDER:
+            v = v + recv3[n]
+        store(n_y + n_x, v)
+        v = sum_y[x]
+        for n in (1, 2, 3):
+            copy_y_back(n).wait_recv()
+        store(0, v + back_y[0] + back_y[1] + back_y[2])
+        copy_x_back(0).wait_recv()
+        store(n_y, sum_x[y_hi] + back_x[...])
 
 
 def shards(wave_count, plane_waves, transmission, wave_index, wave_weight, wave_phase, probe_pos):
@@ -591,8 +655,14 @@
             pltpu.VMEM((3, PROBES * WINDOW, DEPTH // 2), BF16),
             pltpu.VMEM((3, PROBES * WINDOW, DEPTH // 2), BF16),
             pltpu.VMEM((2, PROBES * WINDOW, 2 * LANES), F32),
-            pltpu.VMEM((wave_count, PROBES, 2 * share, LANES), F32),
-            pltpu.VMEM((wave_count, PROBES, 2 * share, LANES), F32),
+            pltpu.VMEM((2, 4, PROBES, 2 * share, LANES), F32),
+            pltpu.VMEM((wave_count, PROBES - sum(ROUTED), 2 * share, LANES), F32),
+            pltpu.VMEM((4, ROUTED[0], 2 * share, LANES), F32),
+            pltpu.VMEM((4, ROUTED[0], 2 * share, LANES), F32),
+            pltpu.VMEM((3, ROUTED[0], 2 * share, LANES), F32),
+            pltpu.VMEM((3, 2, ROUTED[1], 2 * share, LANES), F32),
+            pltpu.VMEM((2, ROUTED[1], 2 * share, LANES), F32),
+            pltpu.VMEM((ROUTED[1], 2 * share, LANES), F32),
             pltpu.SemaphoreType.DMA((len(tables) + 4,)),
             pltpu.SemaphoreType.DMA((2, LANES // ROWS_LOAD)),
             pltpu.SemaphoreType.DMA((chunks, PARTS)),
@@ -601,8 +671,10 @@
             pltpu.SemaphoreType.DMA((chunks, 2, PARTS)),
             pltpu.SemaphoreType.DMA((chunks, PARTS // 2)),
             pltpu.SemaphoreType.DMA((chunks, 2)),
-            pltpu.SemaphoreType.DMA((PROBES // BATCH, wave_count)),
-            pltpu.SemaphoreType.DMA((PROBES // BATCH, wave_count)),
+            pltpu.SemaphoreType.DMA((wave_count,)),
+            pltpu.SemaphoreType.DMA((wave_count,)),
+            pltpu.SemaphoreType.DMA((8,)),
+            pltpu.SemaphoreType.DMA((8,)),
         ],
         compiler_params=pltpu.CompilerParams(
             collective_id=0, has_side_effects=True, vmem_limit_bytes=60 * 1024 * 1024

time: 76 us -> 74.9 us (0.986)
  Pallas kernels: 73.1 us -> 72 us
    pallas_call x1, Pallas kernels: 73.1 us -> 72 us  [shards(): pl.pallas_call(functools.partial(body, wave_count), out_shape=jax.ShapeDt...]
where the time goes in v4:
time: 74.9 us; the launch traced here: 74.7 us
  Pallas kernels  72 us (96%)
  local copies, waits for them, and re-layouts  1.47 us (2%)
  between operations  1.3 us (2%)
    pallas_call x1, Pallas kernels, shards(): pl.pallas_call(functools.partial(body, wave_count), out_shape=jax.ShapeDt...  72 us

profile of v4, /device:TPU:1, one launch (start us, length us, event | category | flops | bytes accessed | tf_op | source)
XLA Modules:
  0.0 74.7 jit_solution(10551387636808508677)
XLA Ops:
  1.3 72.0 %shard_map.154 = f32[8,16,128]{2,1,0:T(8,128)} custom-call(f32[2,1,128,2048]{3,2,1,0:T(8,128)} %pw_hbm.1, f32[1,2,128,2048]{3,2,1,0:T(8,128)} %tr_hbm.1, bf16[176,768]{1,0:T(8,128)(2,1)} %constant.20.clone.fx_hbm, bf16[768,256]{1,0:T(8,128)(2,1)} %constant.21.clone.fy_hbm, bf16[768,256]{1,0:T(8,128)(2,1)} %constant.22.clone.iy_hbm, ...), custom_call_target="tpu_custom_call" | custom-call | tf_op jit(solution)/shard_map/pallas_call | solution.py:632
  73.3 1.5 %copy.20 = f32[8,16,128]{2,1,0:T(8,128)} copy(f32[8,16,128]{2,1,0:T(8,128)} %shard_map.154) | data formatting | bytes 131072
